TPU v7x, 512 devices: a whole 4x4x16 slice. The times are simulated.
512 devices in a mesh: img: 8 (over x, core), cls: 8 (over z_lo), tpl: 8 (over z_hi, y).
Axes of the slice: x: 4, y: 4, z: 16 (z_hi: 2, z_lo: 8; z = z_hi * 8 + z_lo), core: 2. Of those that a mesh axis runs over, the one named last changes fastest.
Arguments:
- images: bfloat16 [16384, 1280], P(('img', 'tpl')), may hold values from -5 to 5
- labels: int32 [16384], P(('img', 'tpl')), may hold values from 0 to 4095
- templates: bfloat16 [32, 4096, 1280], P('tpl', ('cls', 'img')), may hold values from -0.125 to 0.125
- projection: bfloat16 [1280, 1280], P('img', 'cls'), may hold values from -0.08441157 to 0.08441157
Outputs:
- grad_templates: bfloat16 [32, 4096, 1280], P('tpl', ('cls', 'img'))
- grad_projection: float32 [1280, 1280], P('img', 'cls')
All inputs are finite; a program needn't handle non-finite values.
Results may differ from a plain program's by a relative error of at most 0.011.
Values may be sent and summed in bfloat16 or wider, within the bound.
A program may use at most 64 MiB of HBM per device.

v0:
```python
import jax
import jax.numpy as jnp
from jax import lax
from jax.sharding import PartitionSpec as P

logit_scale = 50.0
epsilon = 1e-06


def inverse_norm(values):
    return lax.rsqrt(jnp.sum(values * values, axis=-1, keepdims=True) + epsilon)


def body(images, labels, templates, projection):
    tpl_count = templates.shape[0]
    cls_count = templates.shape[1]
    feat_width = templates.shape[2]
    tpl_total = tpl_count * lax.axis_size("tpl")
    img_count = lax.axis_size("img")
    wide_proj = lax.all_gather(projection, "cls", axis=1, tiled=True)
    full_proj = lax.all_gather(wide_proj, "img", axis=0, tiled=True)
    flat_tpl = templates.reshape(tpl_count * cls_count, feat_width)
    text_z = jnp.dot(flat_tpl, full_proj, preferred_element_type=jnp.float32)
    text_rz = inverse_norm(text_z)
    text_u = text_z * text_rz
    u_three = text_u.reshape(tpl_count, cls_count, feat_width)
    local_sum = jnp.sum(u_three, axis=0)
    mean_emb = lax.psum(local_sum, "tpl") / tpl_total
    mean_rn = inverse_norm(mean_emb)
    class_w = mean_emb * mean_rn
    class_b = class_w.astype(jnp.bfloat16)
    img_f = images.astype(jnp.float32)
    img_b = (img_f * inverse_norm(img_f)).astype(jnp.bfloat16)
    all_img, all_labels = (
        lax.all_gather(img_b, "img", axis=0, tiled=True),
        lax.all_gather(labels, "img", axis=0, tiled=True),
    )
    scores = logit_scale * jnp.einsum(
        "cd,nd->cn", class_b, all_img, preferred_element_type=jnp.float32
    )
    exp_scores = jnp.exp(scores)
    totals = lax.psum(jnp.sum(exp_scores, axis=0), ("img", "cls"))
    first_id = (lax.axis_index("cls") * img_count + lax.axis_index("img")) * cls_count
    class_ids = first_id + lax.broadcasted_iota(jnp.int32, (cls_count, 1), 0)
    one_hot = (all_labels[None, :] == class_ids).astype(jnp.float32)
    grad_logit = (exp_scores / totals[None, :] - one_hot).astype(jnp.bfloat16)
    partial_value = logit_scale * jnp.dot(grad_logit, all_img, preferred_element_type=jnp.float32)
    class_g = lax.psum(partial_value, "tpl")
    dot_wg = jnp.sum(class_w * class_g, axis=1, keepdims=True)
    grad_mean = (class_g - class_w * dot_wg) * mean_rn
    per_u = grad_mean / tpl_total
    inner_prod = jnp.sum(u_three * per_u[None], axis=2, keepdims=True)
    grad_z = (
        (per_u[None] - u_three * inner_prod) * text_rz.reshape(tpl_count, cls_count, 1)
    ).astype(jnp.bfloat16)
    grad_flat = grad_z.reshape(tpl_count * cls_count, feat_width)
    grad_tpl = lax.dot_general(
        grad_flat, full_proj, (((1,), (1,)), ((), ())), preferred_element_type=jnp.float32
    )
    grad_templates = grad_tpl.astype(jnp.bfloat16).reshape(tpl_count, cls_count, feat_width)
    tpl_columns = lax.all_to_all(flat_tpl, "img", split_axis=1, concat_axis=0, tiled=True)
    partial_proj = lax.dot_general(
        tpl_columns,
        lax.all_gather(grad_flat, "img", axis=0, tiled=True),
        (((0,), (0,)), ((), ())),
        preferred_element_type=jnp.float32,
    )
    shared_proj = lax.psum_scatter(
        partial_proj.astype(jnp.bfloat16), "cls", scatter_dimension=1, tiled=True
    )
    grad_projection = lax.psum(shared_proj, "tpl").astype(jnp.float32)
    return (grad_templates, grad_projection)


def solution(mesh):
    in_specs = (
        P(("img", "tpl"), None),
        P(("img", "tpl")),
        P("tpl", ("cls", "img"), None),
        P("img", "cls"),
    )
    out_specs = (P("tpl", ("cls", "img"), None), P("img", "cls"))
    return jax.shard_map(body, mesh=mesh, in_specs=in_specs, out_specs=out_specs, check_vma=False)
```

profile of v0, /device:TPU:6, one launch (start us, length us, event | category | flops | bytes accessed | tf_op | source)
XLA Modules:
  0.0 856.8 jit_solution(12290353934308617125)
XLA Ops:
  7.2 1.0 copy.10
  8.3 51.1 %all_gather.15 = bf16[160,1280]{0,1:T(8,128)(2,1)S(1)} all-gather(bf16[160,160]{0,1:T(8,128)(2,1)S(1)} %copy.10), channel_id=1, replica_groups=mesh['img'=8,'cls'=8,'tpl'=8] {'cls'}, dimensions={1}, use_global_device_ids=true | all-gather | bytes 460800 | tf_op jit(solution)/shard_map/all_gather | solution.py:20
  60.7 36.6 %all-gather.5.cloned.1.call-done = bf16[1280,1280]{1,0:T(8,128)(2,1)} async-done(((bf16[160,1280]{1,0:T(8,128)(2,1)}), bf16[1280,1280]{1,0:T(8,128)(2,1)}) %all-gather.5.cloned.1.call-update) | async-done | bytes 3276816 | tf_op jit(solution)/shard_map/all_gather | solution.py:21
  97.3 3.0 multiply_reduce_fusion
  101.5 1.0 fusion.3
  102.6 8.4 all-gather
  111.0 144.2 %all-reduce.3.cloned.1.call-done = f32[64,1280]{1,0:T(8,128)} async-done(((f32[64,1280]{1,0:T(8,128)}), f32[64,1280]{1,0:T(8,128)}) %all-reduce.3.cloned.1.call-update) | async-done | bytes 327696 | tf_op jit(solution)/shard_map/psum | solution.py:28
  255.2 1.1 multiply_reduce_fusion.2
  256.3 34.3 %all-gather.7.cloned.1.call-done = bf16[2048,1280]{1,0:T(8,128)(2,1)} async-done(((bf16[256,1280]{1,0:T(8,128)(2,1)}), bf16[2048,1280]{1,0:T(8,128)(2,1)}) %all-gather.7.cloned.1.call-update) | async-done | bytes 5242896 | tf_op jit(solution)/shard_map/all_gather | solution.py:35
  290.6 4.3 fusion.11
  294.9 204.1 %psum.29 = f32[2048]{0:T(1024)S(1)} all-reduce(f32[2048]{0:T(1024)S(1)} %get-tuple-element.6), channel_id=1, replica_groups=mesh['img'=8,'cls'=8,'tpl'=8] {'img','cls'}, use_global_device_ids=true, to_apply=%region_6.0 | all-reduce | flops 2048 | bytes 16384 | tf_op jit(solution)/shard_map/psum | solution.py:42
  499.1 4.3 convolution_multiply_fusion
  503.5 164.7 %all-reduce.5.cloned.1.call-done = f32[64,1280]{1,0:T(8,128)} async-done(((f32[64,1280]{1,0:T(8,128)}), f32[64,1280]{1,0:T(8,128)}) %all-reduce.5.cloned.1.call-update) | async-done | bytes 327696 | tf_op jit(solution)/shard_map/psum | solution.py:48
  668.1 1.2 multiply_reduce_fusion.1
  669.3 1.1 multiply_multiply_fusion
  670.7 1.1 fusion.6
  671.9 1.3 all_to_all.14
  674.2 20.7 %all_to_all.19 = bf16[256,8,160]{0,2,1:T(8,128)(2,1)S(1)} all-to-all(bf16[256,8,160]{0,2,1:T(8,128)(2,1)S(1)} %copy.12), channel_id=1, replica_groups=mesh['img'=8,'cls'=8,'tpl'=8] {'img'}, dimensions={1} | all-to-all | bytes 1310720 | tf_op jit(solution)/shard_map/all_to_all | solution.py:61
  695.0 15.7 %all-gather.9.cloned.1.call-done = bf16[2048,1280]{1,0:T(8,128)(2,1)} async-done(((bf16[256,1280]{1,0:T(8,128)(2,1)}), bf16[2048,1280]{1,0:T(8,128)(2,1)}) %all-gather.9.cloned.1.call-update) | async-done | bytes 5242896 | tf_op jit(solution)/shard_map/all_gather | solution.py:64
  710.7 3.5 fusion
  714.2 1.1 copy.14
  715.3 3.8 convolution_convert_fusion
  719.1 57.3 %reduce-scatter.4.cloned.1.call-done = bf16[160,160]{1,0:T(8,128)(2,1)} async-done(((bf16[1280,160]{1,0:T(8,128)(2,1)}), bf16[160,160]{1,0:T(8,128)(2,1)}) %reduce-scatter.4.cloned.1.call-update) | async-done | bytes 51216
  777.4 71.8 %psum.31 = bf16[160,160]{1,0:T(8,128)(2,1)S(1)} all-reduce(bf16[160,160]{1,0:T(8,128)(2,1)S(1)} %copy.15), channel_id=1, replica_groups=mesh['img'=8,'cls'=8,'tpl'=8] {'tpl'}, use_global_device_ids=true, to_apply=%region_11.0 | all-reduce | flops 25600 | bytes 102400 | tf_op jit(solution)/shard_map/psum | solution.py:71
  (37 shorter events, 5.6 us)
Async XLA Ops:
  7.2 53.3 %copy-start.1 = (bf16[256,1280]{1,0:T(8,128)(2,1)S(1)}, bf16[256,1280]{1,0:T(8,128)(2,1)}, u32[]{:S(2)}) copy-start(bf16[256,1280]{1,0:T(8,128)(2,1)} %param.4) | copy-start | bytes 1966084
  7.2 90.2 %all-gather.5.cloned.1.call-start = ((), (), s32[]{:S(2)}) async-start(), calls=%async_computation.2 | async-start | bytes 3686400 | tf_op jit(solution)/shard_map/all_gather | solution.py:21
  8.3 89.1 %copy-start.3 = (bf16[4,64,1280]{2,1,0:T(8,128)(2,1)S(1)}, bf16[4,64,1280]{2,1,0:T(8,128)(2,1)}, u32[]{:S(2)}) copy-start(bf16[4,64,1280]{2,1,0:T(8,128)(2,1)} %param.6) | copy-start | bytes 1966084
  60.4 194.7 %all-reduce.3.cloned.1.call-start = ((), (), s32[]{:S(2)}) async-start(), calls=%async_computation.3 | async-start | bytes 655360 | tf_op jit(solution)/shard_map/psum | solution.py:28
  101.4 1.2 copy-start.5
  101.4 189.1 %all-gather.7.cloned.1.call-start = ((), (), s32[]{:S(2)}) async-start(), calls=%async_computation.4 | async-start | bytes 5898240 | tf_op jit(solution)/shard_map/all_gather | solution.py:35
  102.5 565.6 %all-reduce.5.cloned.1.call-start = ((), (), s32[]{:S(2)}) async-start(), calls=%async_computation.5 | async-start | bytes 655360 | tf_op jit(solution)/shard_map/psum | solution.py:48
  499.1 169.1 %copy-start = (f32[64,1280]{1,0:T(8,128)S(1)}, f32[64,1280]{1,0:T(8,128)}, u32[]{:S(2)}) copy-start(f32[64,1280]{1,0:T(8,128)} %all-reduce.3.cloned.1.call-done) | copy-start | bytes 983044
  503.4 207.3 %all-gather.9.cloned.1.call-start = ((), (), s32[]{:S(2)}) async-start(), calls=%async_computation.6 | async-start | bytes 5898240 | tf_op jit(solution)/shard_map/all_gather | solution.py:64
  670.7 1.2 copy-start.4
  671.9 104.6 %reduce-scatter.4.cloned.1.call-start = ((), (), s32[]{:S(2)}) async-start(), calls=%async_computation.7 | async-start | bytes 737280
  714.2 1.1 copy-start.2
Sparse Core Ops, SparseCore 0:
  60.5 36.7 all-gather.4
  101.5 153.5 all-reduce.2
  258.1 32.4 all-gather.6
  503.5 164.5 all-reduce.4
  672.0 38.6 all-gather.8
  715.4 60.9 reduce-scatter.3
where the time goes:
time: 857 us
  waiting for transfers between devices  453 us (53%)
  blocking collectives  356 us (42%)
  matrix products  19 us (2%)
  between operations  14.3 us (2%)
    psum x1, blocking collectives, body(): totals = lax.psum(jnp.sum(exp_scores, axis=0), ('img', 'cls'))  204 us
    psum x1, waiting for transfers between devices, body(): class_g = lax.psum(partial_value, 'tpl')  165 us
    psum x1, waiting for transfers between devices, body(): mean_emb = lax.psum(local_sum, 'tpl') / tpl_total  144 us
    psum x1, blocking collectives, body(): grad_projection = lax.psum(shared_proj, 'tpl').astype(jnp.float32)  71.8 us
    unnamed x7, waiting for transfers between devices  57.4 us
    all_gather x1, blocking collectives, body(): wide_proj = lax.all_gather(projection, 'cls', axis=1, tiled=True)  51.1 us
    all_gather x1, waiting for transfers between devices, body(): full_proj = lax.all_gather(wide_proj, 'img', axis=0, tiled=True)  36.6 us
    all_gather x1, waiting for transfers between devices, body(): lax.all_gather(img_b, 'img', axis=0, tiled=True)  34.3 us
  transfers between devices with their start and end apart: 6, of which 6 were waited for; matrix products, arithmetic and copies ran while one was open for 1% of the time, Pallas kernels for 0%

commit v1 on v0

--- a/solution.py
+++ b/solution.py
@@ -39,7 +39,7 @@
         "cd,nd->cn", class_b, all_img, preferred_element_type=jnp.float32
     )
     exp_scores = jnp.exp(scores)
-    totals = lax.psum(jnp.sum(exp_scores, axis=0), ("img", "cls"))
+    totals = lax.psum(lax.psum(jnp.sum(exp_scores, axis=0), "img"), "cls")
     first_id = (lax.axis_index("cls") * img_count + lax.axis_index("img")) * cls_count
     class_ids = first_id + lax.broadcasted_iota(jnp.int32, (cls_count, 1), 0)
     one_hot = (all_labels[None, :] == class_ids).astype(jnp.float32)

time: 857 us -> 682 us (0.80)
  blocking collectives: 356 us -> 198 us
  waiting for transfers between devices: 453 us -> 436 us
    psum x1 -> x2, blocking collectives: 204 us -> 45.7 us  [body(): totals = lax.psum(lax.psum(jnp.sum(exp_scores, axis=0), 'img'), 'cls')]
    psum x1, waiting for transfers between devices: 165 us -> 148 us  [body(): class_g = lax.psum(partial_value, 'tpl')]
where the time goes in v1:
time: 682 us; the launch traced here: 681 us
  waiting for transfers between devices  436 us (64%)
  blocking collectives  198 us (29%)
  matrix products  19 us (3%)
  between operations  14.3 us (2%)
  other arithmetic  7.75 us (1%)
    psum x1, waiting for transfers between devices, body(): class_g = lax.psum(partial_value, 'tpl')  148 us
    psum x1, waiting for transfers between devices, body(): mean_emb = lax.psum(local_sum, 'tpl') / tpl_total  144 us
    psum x1, blocking collectives, body(): grad_projection = lax.psum(shared_proj, 'tpl').astype(jnp.float32)  71.6 us
    unnamed x7, waiting for transfers between devices  57.4 us
    all_gather x1, blocking collectives, body(): wide_proj = lax.all_gather(projection, 'cls', axis=1, tiled=True)  51.1 us
    psum x2, blocking collectives, body(): totals = lax.psum(lax.psum(jnp.sum(exp_scores, axis=0), 'img'), 'cls')  45.7 us
    all_gather x1, waiting for transfers between devices, body(): full_proj = lax.all_gather(wide_proj, 'img', axis=0, tiled=True)  36.6 us
    all_gather x1, waiting for transfers between devices, body(): lax.all_gather(img_b, 'img', axis=0, tiled=True)  34.3 us
  transfers between devices with their start and end apart: 6, of which 6 were waited for; matrix products, arithmetic and copies ran while one was open for 1% of the time, Pallas kernels for 0%

profile of v1, /device:TPU:6, one launch (start us, length us, event | category | flops | bytes accessed | tf_op | source)
XLA Modules:
  0.0 681.0 jit_solution(14284836278866557815)
XLA Ops:
  7.2 1.0 copy.10
  8.3 51.1 %all_gather.15 = bf16[160,1280]{0,1:T(8,128)(2,1)S(1)} all-gather(bf16[160,160]{0,1:T(8,128)(2,1)S(1)} %copy.10), channel_id=1, replica_groups=mesh['img'=8,'cls'=8,'tpl'=8] {'cls'}, dimensions={1}, use_global_device_ids=true | all-gather | bytes 460800 | tf_op jit(solution)/shard_map/all_gather | solution.py:20
  60.7 36.6 %all-gather.5.cloned.1.call-done = bf16[1280,1280]{1,0:T(8,128)(2,1)} async-done(((bf16[160,1280]{1,0:T(8,128)(2,1)}), bf16[1280,1280]{1,0:T(8,128)(2,1)}) %all-gather.5.cloned.1.call-update) | async-done | bytes 3276816 | tf_op jit(solution)/shard_map/all_gather | solution.py:21
  97.3 3.0 multiply_reduce_fusion
  102.6 8.4 %all-gather = s32[8,1,256]{2,1,0:T(1,128)S(1)} all-gather(s32[1,1,256]{2,1,0:T(1,128)S(1)} %bitcast.36), channel_id=1, replica_groups=mesh['img'=8,'cls'=8,'tpl'=8] {'img'}, dimensions={0}, use_global_device_ids=true | all-gather | bytes 9216 | tf_op jit(solution)/shard_map/all_gather | solution.py:36
  111.0 144.2 %all-reduce.3.cloned.1.call-done = f32[64,1280]{1,0:T(8,128)} async-done(((f32[64,1280]{1,0:T(8,128)}), f32[64,1280]{1,0:T(8,128)}) %all-reduce.3.cloned.1.call-update) | async-done | bytes 327696 | tf_op jit(solution)/shard_map/psum | solution.py:28
  255.2 1.1 multiply_reduce_fusion.2
  256.3 34.3 %all-gather.7.cloned.1.call-done = bf16[2048,1280]{1,0:T(8,128)(2,1)} async-done(((bf16[256,1280]{1,0:T(8,128)(2,1)}), bf16[2048,1280]{1,0:T(8,128)(2,1)}) %all-gather.7.cloned.1.call-update) | async-done | bytes 5242896 | tf_op jit(solution)/shard_map/all_gather | solution.py:35
  290.6 4.3 fusion.11
  294.9 11.6 %psum.36 = f32[2048]{0:T(1024)S(1)} all-reduce(f32[2048]{0:T(1024)S(1)} %get-tuple-element.6), channel_id=1, replica_groups=mesh['img'=8,'cls'=8,'tpl'=8] {'img'}, use_global_device_ids=true, to_apply=%region_6.0 | all-reduce | flops 2048 | bytes 16384 | tf_op jit(solution)/shard_map/psum | solution.py:42
  306.5 34.1 %psum.37 = f32[2048]{0:T(1024)S(1)} all-reduce(f32[2048]{0:T(1024)S(1)} %psum.36), channel_id=1, replica_groups=mesh['img'=8,'cls'=8,'tpl'=8] {'cls'}, use_global_device_ids=true, to_apply=%region_7.0 | all-reduce | flops 2048 | bytes 16384 | tf_op jit(solution)/shard_map/psum | solution.py:42
  340.6 4.3 convolution_multiply_fusion
  345.0 147.5 %all-reduce.5.cloned.1.call-done = f32[64,1280]{1,0:T(8,128)} async-done(((f32[64,1280]{1,0:T(8,128)}), f32[64,1280]{1,0:T(8,128)}) %all-reduce.5.cloned.1.call-update) | async-done | bytes 327696 | tf_op jit(solution)/shard_map/psum | solution.py:48
  492.5 1.2 multiply_reduce_fusion.1
  493.7 1.1 multiply_multiply_fusion
  495.1 1.1 fusion.6
  496.3 1.3 all_to_all.14
  498.7 20.7 %all_to_all.19 = bf16[256,8,160]{0,2,1:T(8,128)(2,1)S(1)} all-to-all(bf16[256,8,160]{0,2,1:T(8,128)(2,1)S(1)} %copy.12), channel_id=1, replica_groups=mesh['img'=8,'cls'=8,'tpl'=8] {'img'}, dimensions={1} | all-to-all | bytes 1310720 | tf_op jit(solution)/shard_map/all_to_all | solution.py:61
  519.4 15.7 %all-gather.9.cloned.1.call-done = bf16[2048,1280]{1,0:T(8,128)(2,1)} async-done(((bf16[256,1280]{1,0:T(8,128)(2,1)}), bf16[2048,1280]{1,0:T(8,128)(2,1)}) %all-gather.9.cloned.1.call-update) | async-done | bytes 5242896 | tf_op jit(solution)/shard_map/all_gather | solution.py:64
  535.1 3.5 fusion
  538.6 1.1 copy.14
  539.7 3.8 convolution_convert_fusion
  543.6 57.3 %reduce-scatter.4.cloned.1.call-done = bf16[160,160]{1,0:T(8,128)(2,1)} async-done(((bf16[1280,160]{1,0:T(8,128)(2,1)}), bf16[160,160]{1,0:T(8,128)(2,1)}) %reduce-scatter.4.cloned.1.call-update) | async-done | bytes 51216
  601.9 71.6 %psum.39 = bf16[160,160]{1,0:T(8,128)(2,1)S(1)} all-reduce(bf16[160,160]{1,0:T(8,128)(2,1)S(1)} %copy.15), channel_id=1, replica_groups=mesh['img'=8,'cls'=8,'tpl'=8] {'tpl'}, use_global_device_ids=true, to_apply=%region_12.0 | all-reduce | flops 25600 | bytes 102400 | tf_op jit(solution)/shard_map/psum | solution.py:71
  (38 shorter events, 6.6 us)
Async XLA Ops:
  7.2 53.3 %copy-start.1 = (bf16[256,1280]{1,0:T(8,128)(2,1)S(1)}, bf16[256,1280]{1,0:T(8,128)(2,1)}, u32[]{:S(2)}) copy-start(bf16[256,1280]{1,0:T(8,128)(2,1)} %param.4) | copy-start | bytes 1966084
  7.2 90.2 %all-gather.5.cloned.1.call-start = ((), (), s32[]{:S(2)}) async-start(), calls=%async_computation.2 | async-start | bytes 3686400 | tf_op jit(solution)/shard_map/all_gather | solution.py:21
  8.3 89.1 %copy-start.3 = (bf16[4,64,1280]{2,1,0:T(8,128)(2,1)S(1)}, bf16[4,64,1280]{2,1,0:T(8,128)(2,1)}, u32[]{:S(2)}) copy-start(bf16[4,64,1280]{2,1,0:T(8,128)(2,1)} %param.6) | copy-start | bytes 1966084
  60.4 194.7 %all-reduce.3.cloned.1.call-start = ((), (), s32[]{:S(2)}) async-start(), calls=%async_computation.3 | async-start | bytes 655360 | tf_op jit(solution)/shard_map/psum | solution.py:28
  101.4 1.2 copy-start.5
  101.4 189.1 %all-gather.7.cloned.1.call-start = ((), (), s32[]{:S(2)}) async-start(), calls=%async_computation.4 | async-start | bytes 5898240 | tf_op jit(solution)/shard_map/all_gather | solution.py:35
  102.5 390.0 %all-reduce.5.cloned.1.call-start = ((), (), s32[]{:S(2)}) async-start(), calls=%async_computation.5 | async-start | bytes 655360 | tf_op jit(solution)/shard_map/psum | solution.py:48
  340.6 151.9 %copy-start = (f32[64,1280]{1,0:T(8,128)S(1)}, f32[64,1280]{1,0:T(8,128)}, u32[]{:S(2)}) copy-start(f32[64,1280]{1,0:T(8,128)} %all-reduce.3.cloned.1.call-done) | copy-start | bytes 983044
  345.0 190.1 %all-gather.9.cloned.1.call-start = ((), (), s32[]{:S(2)}) async-start(), calls=%async_computation.6 | async-start | bytes 5898240 | tf_op jit(solution)/shard_map/all_gather | solution.py:64
  495.1 1.2 copy-start.4
  496.3 104.6 %reduce-scatter.4.cloned.1.call-start = ((), (), s32[]{:S(2)}) async-start(), calls=%async_computation.7 | async-start | bytes 737280
  538.6 1.1 copy-start.2
Sparse Core Ops, SparseCore 0:
  60.5 36.7 all-gather.4
  101.5 153.5 all-reduce.2
  258.1 32.4 all-gather.6
  345.1 147.3 all-reduce.4
  496.4 38.6 all-gather.8
  539.9 60.9 reduce-scatter.3

commit v2 on v0

--- a/solution.py
+++ b/solution.py
@@ -17,7 +17,9 @@
     feat_width = templates.shape[2]
     tpl_total = tpl_count * lax.axis_size("tpl")
     img_count = lax.axis_size("img")
-    wide_proj = lax.all_gather(projection, "cls", axis=1, tiled=True)
+    wide_proj = jnp.concatenate(
+        lax.all_to_all(jnp.stack([projection] * lax.axis_size("cls")), "cls", 0, 0), axis=1
+    )
     full_proj = lax.all_gather(wide_proj, "img", axis=0, tiled=True)
     flat_tpl = templates.reshape(tpl_count * cls_count, feat_width)
     text_z = jnp.dot(flat_tpl, full_proj, preferred_element_type=jnp.float32)

time: 857 us -> 848 us (0.989)
    all_gather x1 -> x0, blocking collectives: 51.1 us -> none  [body(): wide_proj = lax.all_gather(projection, 'cls', axis=1, tiled=True)]
    all_to_all x0 -> x1, blocking collectives: none -> 46.7 us  [body(): lax.all_to_all(jnp.stack([projection] * lax.axis_size('cls')), 'cls', 0, 0)]
where the time goes in v2:
time: 848 us
  waiting for transfers between devices  448 us (53%)
  blocking collectives  352 us (42%)
  matrix products  19 us (2%)
  between operations  14.3 us (2%)
    psum x1, blocking collectives, body(): totals = lax.psum(jnp.sum(exp_scores, axis=0), ('img', 'cls'))  204 us
    psum x1, waiting for transfers between devices, body(): class_g = lax.psum(partial_value, 'tpl')  165 us
    psum x1, waiting for transfers between devices, body(): mean_emb = lax.psum(local_sum, 'tpl') / tpl_total  144 us
    psum x1, blocking collectives, body(): grad_projection = lax.psum(shared_proj, 'tpl').astype(jnp.float32)  71.7 us
    unnamed x7, waiting for transfers between devices  57.4 us
    all_to_all x1, blocking collectives, body(): lax.all_to_all(jnp.stack([projection] * lax.axis_size('cls')), 'cls', 0, 0)  46.7 us
    all_gather x1, waiting for transfers between devices, body(): lax.all_gather(img_b, 'img', axis=0, tiled=True)  34.3 us
    all_gather x1, waiting for transfers between devices, body(): full_proj = lax.all_gather(wide_proj, 'img', axis=0, tiled=True)  31.5 us
  transfers between devices with their start and end apart: 6, of which 6 were waited for; matrix products, arithmetic and copies ran while one was open for 1% of the time, Pallas kernels for 0%

profile of v2, /device:TPU:6, one launch (start us, length us, event | category | flops | bytes accessed | tf_op | source)
XLA Modules:
  0.0 847.9 jit_solution(10681312841360047048)
XLA Ops:
  8.1 46.7 %all_to_all.24 = bf16[8,160,160]{2,1,0:T(8,128)(2,1)S(1)} all-to-all(bf16[8,160,160]{2,1,0:T(8,128)(2,1)S(1)} %stack.2), channel_id=1, replica_groups=mesh['img'=8,'cls'=8,'tpl'=8] {'cls'}, dimensions={0} | all-to-all | bytes 819200 | tf_op jit(solution)/shard_map/all_to_all | solution.py:21
  55.2 1.5 reshape.70
  57.0 31.5 %all-gather.5.cloned.1.call-done = bf16[1280,1280]{1,0:T(8,128)(2,1)} async-done(((bf16[160,1280]{1,0:T(8,128)(2,1)}), bf16[1280,1280]{1,0:T(8,128)(2,1)}) %all-gather.5.cloned.1.call-update) | async-done | bytes 3276816 | tf_op jit(solution)/shard_map/all_gather | solution.py:23
  88.4 3.0 multiply_reduce_fusion
  92.6 1.0 fusion.3
  93.7 8.4 all-gather
  102.1 144.3 %all-reduce.3.cloned.1.call-done = f32[64,1280]{1,0:T(8,128)} async-done(((f32[64,1280]{1,0:T(8,128)}), f32[64,1280]{1,0:T(8,128)}) %all-reduce.3.cloned.1.call-update) | async-done | bytes 327696 | tf_op jit(solution)/shard_map/psum | solution.py:30
  246.4 1.1 multiply_reduce_fusion.2
  247.5 34.3 %all-gather.7.cloned.1.call-done = bf16[2048,1280]{1,0:T(8,128)(2,1)} async-done(((bf16[256,1280]{1,0:T(8,128)(2,1)}), bf16[2048,1280]{1,0:T(8,128)(2,1)}) %all-gather.7.cloned.1.call-update) | async-done | bytes 5242896 | tf_op jit(solution)/shard_map/all_gather | solution.py:37
  281.8 4.3 fusion.11
  286.1 204.1 %psum.29 = f32[2048]{0:T(1024)S(1)} all-reduce(f32[2048]{0:T(1024)S(1)} %get-tuple-element.6), channel_id=1, replica_groups=mesh['img'=8,'cls'=8,'tpl'=8] {'img','cls'}, use_global_device_ids=true, to_apply=%region_6.0 | all-reduce | flops 2048 | bytes 16384 | tf_op jit(solution)/shard_map/psum | solution.py:44
  490.2 4.3 convolution_multiply_fusion
  494.6 164.7 %all-reduce.5.cloned.1.call-done = f32[64,1280]{1,0:T(8,128)} async-done(((f32[64,1280]{1,0:T(8,128)}), f32[64,1280]{1,0:T(8,128)}) %all-reduce.5.cloned.1.call-update) | async-done | bytes 327696 | tf_op jit(solution)/shard_map/psum | solution.py:50
  659.3 1.2 multiply_reduce_fusion.1
  660.5 1.1 multiply_multiply_fusion
  661.9 1.1 fusion.6
  663.2 1.3 all_to_all.18
  665.5 20.7 %all_to_all.25 = bf16[256,8,160]{0,2,1:T(8,128)(2,1)S(1)} all-to-all(bf16[256,8,160]{0,2,1:T(8,128)(2,1)S(1)} %copy.8), channel_id=1, replica_groups=mesh['img'=8,'cls'=8,'tpl'=8] {'img'}, dimensions={1} | all-to-all | bytes 1310720 | tf_op jit(solution)/shard_map/all_to_all | solution.py:63
  686.2 15.7 %all-gather.9.cloned.1.call-done = bf16[2048,1280]{1,0:T(8,128)(2,1)} async-done(((bf16[256,1280]{1,0:T(8,128)(2,1)}), bf16[2048,1280]{1,0:T(8,128)(2,1)}) %all-gather.9.cloned.1.call-update) | async-done | bytes 5242896 | tf_op jit(solution)/shard_map/all_gather | solution.py:66
  701.9 3.5 fusion
  705.4 1.1 copy.10
  706.5 3.8 convolution_convert_fusion
  710.4 57.3 %reduce-scatter.4.cloned.1.call-done = bf16[160,160]{1,0:T(8,128)(2,1)} async-done(((bf16[1280,160]{1,0:T(8,128)(2,1)}), bf16[160,160]{1,0:T(8,128)(2,1)}) %reduce-scatter.4.cloned.1.call-update) | async-done | bytes 51216
  768.6 71.7 %psum.31 = bf16[160,160]{1,0:T(8,128)(2,1)S(1)} all-reduce(bf16[160,160]{1,0:T(8,128)(2,1)S(1)} %copy.11), channel_id=1, replica_groups=mesh['img'=8,'cls'=8,'tpl'=8] {'tpl'}, use_global_device_ids=true, to_apply=%region_11.0 | all-reduce | flops 25600 | bytes 102400 | tf_op jit(solution)/shard_map/psum | solution.py:73
  (38 shorter events, 5.9 us)
Async XLA Ops:
  7.2 81.3 %all-gather.5.cloned.1.call-start = ((), (), s32[]{:S(2)}) async-start(), calls=%async_computation.3 | async-start | bytes 3686400 | tf_op jit(solution)/shard_map/all_gather | solution.py:23
  54.8 1.9 copy-start.1
  55.2 33.2 %copy-start.3 = (bf16[4,64,1280]{2,1,0:T(8,128)(2,1)S(1)}, bf16[4,64,1280]{2,1,0:T(8,128)(2,1)}, u32[]{:S(2)}) copy-start(bf16[4,64,1280]{2,1,0:T(8,128)(2,1)} %param.6) | copy-start | bytes 1966084
  56.7 189.7 %all-reduce.3.cloned.1.call-start = ((), (), s32[]{:S(2)}) async-start(), calls=%async_computation.4 | async-start | bytes 655360 | tf_op jit(solution)/shard_map/psum | solution.py:30
  92.5 1.2 copy-start.5
  92.5 189.3 %all-gather.7.cloned.1.call-start = ((), (), s32[]{:S(2)}) async-start(), calls=%async_computation.5 | async-start | bytes 5898240 | tf_op jit(solution)/shard_map/all_gather | solution.py:37
  93.6 565.7 %all-reduce.5.cloned.1.call-start = ((), (), s32[]{:S(2)}) async-start(), calls=%async_computation.6 | async-start | bytes 655360 | tf_op jit(solution)/shard_map/psum | solution.py:50
  490.2 169.1 %copy-start = (f32[64,1280]{1,0:T(8,128)S(1)}, f32[64,1280]{1,0:T(8,128)}, u32[]{:S(2)}) copy-start(f32[64,1280]{1,0:T(8,128)} %all-reduce.3.cloned.1.call-done) | copy-start | bytes 983044
  494.6 207.3 %all-gather.9.cloned.1.call-start = ((), (), s32[]{:S(2)}) async-start(), calls=%async_computation.7 | async-start | bytes 5898240 | tf_op jit(solution)/shard_map/all_gather | solution.py:66
  661.9 1.2 copy-start.4
  663.1 104.5 %reduce-scatter.4.cloned.1.call-start = ((), (), s32[]{:S(2)}) async-start(), calls=%async_computation.8 | async-start | bytes 737280
  705.4 1.1 copy-start.2
Sparse Core Ops, SparseCore 0:
  56.8 31.5 all-gather.4
  92.6 153.6 all-reduce.2
  249.3 32.4 all-gather.6
  494.7 164.5 all-reduce.4
  663.2 38.6 all-gather.8
  706.7 60.9 reduce-scatter.3
